TPU v7x, 256 devices: a whole 4x4x8 slice. The times are simulated.
256 devices in a mesh: cand: 32 (over z, x_hi, core), query: 8 (over y, x_lo).
Axes of the slice: x: 4 (x_hi: 2, x_lo: 2; x = x_hi * 2 + x_lo), y: 4, z: 8, core: 2. Of those that a mesh axis runs over, the one named last changes fastest.
Arguments:
- pool: bfloat16 [327680, 4096], P(('cand', 'query')), may hold values from -6 to 6
- cand_ids: int32 [262144], P(('cand', 'query')), may hold values from 0 to 1279
- pick_ids: int32 [256], P(('cand', 'query')), may hold values from 0 to 1279
- queries: bfloat16 [1024, 4096], P('query'), may hold values from -6 to 6
Outputs:
- gains: float32 [262144], P(('cand', 'query'))
- coverage: float32 [1024], P('query')
Inputs may be any that keep to these rules, and one draw needn't show every extreme that they name: `cand_ids`: each id is a row within the pool block of 1280 rows that lies on the same device as the id. `pick_ids`: each id is a row within the pool block of 1280 rows that lies on the same device as the id.
All inputs are finite; a program needn't handle non-finite values.
Results may differ from a plain program's by a relative error of at most 0.0003.
Values may be sent and summed in bfloat16 or wider, within the bound.
A program may use at most 128 MiB of HBM per device.

v0:
```python
import math

import jax
import jax.numpy as jnp
from jax import lax
from jax.sharding import PartitionSpec as P

D = 4096


def similarity(rows, targets):
    product = lax.dot_general(
        rows, targets, (((1,), (1,)), ((), ())), preferred_element_type=jnp.float32
    )
    return product * (1.0 / math.sqrt(D))


def on_device(pool, cand_ids, pick_ids, queries):
    q_rows = queries.shape[0]
    candidates = jnp.take(pool, cand_ids, axis=0)
    picked = jnp.take(pool, pick_ids, axis=0)
    best = jnp.max(similarity(picked, lax.all_gather(queries, "query", axis=0, tiled=True)), axis=0)
    coverage = lax.pmax(best, ("cand", "query"))
    scores = similarity(candidates, lax.all_gather(queries, "query", axis=0, tiled=True))
    summed = jnp.sum(jnp.maximum(scores - coverage[None, :], 0.0), axis=1)
    highest = jnp.max(scores, axis=1)
    gained, highest = (summed, highest)
    gains = gained + 1.0 * highest
    own_cover = lax.dynamic_slice_in_dim(coverage, lax.axis_index("query") * q_rows, q_rows, 0)
    return (gains, own_cover)


def solution(mesh):
    in_specs = (
        P(("cand", "query"), None),
        P(("cand", "query")),
        P(("cand", "query")),
        P("query", None),
    )
    out_specs = (P(("cand", "query")), P("query"))
    return jax.shard_map(
        on_device, mesh=mesh, in_specs=in_specs, out_specs=out_specs, check_vma=False
    )
```

profile of v0, /device:TPU:1, one launch (start us, length us, event | category | flops | bytes accessed | tf_op | source)
XLA Modules:
  0.0 289.6 jit_solution(9840144230688379717)
XLA Ops:
  7.2 0.0 all-gather.2.cloned.1.call-start
  7.2 0.7 all-gather.2.cloned.1.call-update
  8.6 0.7 fusion.9
  9.2 0.0 copy-start
  9.3 20.4 %gather_fusion = bf16[1024,4096]{1,0:T(8,128)(2,1)} fusion(bf16[1280,4096]{1,0:T(8,128)(2,1)} %param.4, s32[1024]{0:T(1024)S(1)} %fusion.9), kind=kCustom, calls=%fused_computation | custom fusion | bytes 16781312 | tf_op jit(solution)/shard_map/jit(_take)/gather | solution.py:20
  29.7 0.0 copy-done
  29.7 154.8 %all-gather.2.cloned.1.call-done = bf16[1024,4096]{1,0:T(8,128)(2,1)} async-done(((bf16[128,4096]{1,0:T(8,128)(2,1)}), bf16[1024,4096]{1,0:T(8,128)(2,1)}) %all-gather.2.cloned.1.call-update) | async-done | bytes 8388624 | tf_op jit(solution)/shard_map/all_gather | solution.py:24
  184.5 5.7 %fusion.5 = f32[1,1024]{1,0:T(1,128)S(1)} fusion(bf16[1024,4096]{1,0:T(8,128)(2,1)} %all-gather.2.cloned.1.call-done, pred[]{:T(512)} %bitcast, bf16[1280,4096]{1,0:T(8,128)(2,1)} %param.4, s32[]{:T(128)} %bitcast.1), kind=kOutput, calls=%fused_computation.9 | convolution fusion | flops 8392704 | bytes 8410112 | tf_op jit(solution)/shard_map/dot_general | solution.py:12
  190.2 77.0 %pmax.7 = f32[1024]{0:T(1024)S(1)} all-reduce(f32[1024]{0:T(1024)S(1)} %broadcast_multiply_fusion), channel_id=1, replica_groups=mesh['cand'=32,'query'=8] {'cand','query'}, use_global_device_ids=true, to_apply=%region_0.1 | all-reduce | flops 1024 | bytes 8192 | tf_op jit(solution)/shard_map/pmax | solution.py:23
  267.2 0.6 dynamic_slice.3
  267.8 14.3 %multiply_reduce_fusion = (f32[1024]{0:T(1024)S(1)}, f32[1024]{0:T(1024)S(1)}) fusion(f32[1024]{0:T(1024)S(1)} %pmax.7, bf16[1024,4096]{1,0:T(8,128)(2,1)} %all-gather.2.cloned.1.call-done, bf16[1024,4096]{1,0:T(8,128)(2,1)} %gather_fusion, pred[1024]{0:T(1024)(128)(4,1)S(1)} %compare_and_fusion), kind=kOutput, calls=%fused_computation.6 | convolution fusion | flops 8599369728 | bytes 16790528 | tf_op jit(solution)/shard_map/dot_general | solution.py:12
  282.1 0.6 add.21
  (2 shorter events, 0.0 us)
Async XLA Ops:
  7.2 177.3 %all-gather.2.cloned.1.call-start = ((), (), s32[]{:S(2)}) async-start(), calls=%async_computation | async-start | bytes 9437184 | tf_op jit(solution)/shard_map/all_gather | solution.py:24
  9.2 20.4 %copy-start = (s32[1024]{0:T(1024)S(1)}, s32[1024]{0:T(1024)}, u32[]{:S(2)}) copy-start(s32[1024]{0:T(1024)} %param.5) | copy-start | bytes 12292
Sparse Core Ops, SparseCore 0:
  9.8 174.6 all-gather.1
where the time goes:
time: 290 us
  waiting for transfers between devices  155 us (53%)
  blocking collectives  77 us (27%)
  local copies, waits for them, and re-layouts  21 us (7%)
  matrix products  20 us (7%)
  between operations  14.7 us (5%)
    all_gather x1, waiting for transfers between devices, on_device(): lax.all_gather(queries, 'query', axis=0, tiled=True)  155 us
    pmax x1, blocking collectives, on_device(): coverage = lax.pmax(best, ('cand', 'query'))  77 us
    gather x1, local copies, waits for them, and re-layouts, on_device(): candidates = jnp.take(pool, cand_ids, axis=0)  20.4 us
    dot_general x2, matrix products, similarity(): lax.dot_general(rows, targets, (((1,), (1,)), ((), ())), preferred_elemen...  20 us
  transfers between devices with their start and end apart: 1, of which 1 were waited for; matrix products, arithmetic and copies ran while one was open for 7% of the time, Pallas kernels for 0%

commit v1 on v0

v1 whole, which is shorter than its diff:
```python
import jax
import jax.numpy as jnp
from jax import lax
from jax.experimental import pallas as pl
from jax.experimental.pallas import tpu as pltpu
from jax.sharding import PartitionSpec as P

MESH = pl.DeviceIdType.MESH
D = 4096
TILE = 128
BLOCK = 128
POOL = 1280
SCALE = 1.0 / 64.0
OWN, X, YP, YM, XP, XM, Y2, X2 = range(8)
DELTA = {X: (0, 1), YP: (1, 0), YM: (3, 0), XP: (1, 1), XM: (3, 1), Y2: (2, 0), X2: (2, 1)}


def where_am_i():
    cand, query = lax.axis_index("cand"), lax.axis_index("query")
    core = lax.rem(cand, 2)
    x = lax.rem(lax.div(cand, 2), 2) * 2 + lax.rem(query, 2)
    return x, lax.div(query, 2), lax.div(cand, 4), core


def device(x, y, z, core):
    return ((z * 2 + lax.div(x, 2)) * 2 + core, y * 2 + lax.rem(x, 2))


def dot(a, b):
    return lax.dot_general(a, b, (((1,), (1,)), ((), ())), preferred_element_type=jnp.float32)


def gather_and_score(
    pick_ref, pool_ref, q_ref, part_ref, cover_ref,
    allq, pool, scores, pick_f32, pick_buf, pick_rows, cover_x, cover_z, cover_q, columns,
    local_sem, send_sem, recv_sem,
):
    x, y, z, core = where_am_i()
    odd = lax.rem(z, 2)
    x_pair = x + 1 - 2 * lax.rem(x, 2)

    def step(v, by, size):
        return lax.rem(v + by + size, size)

    target = {
        "x+": device(step(x, 1, 4), y, z, core),
        "x-": device(step(x, -1, 4), y, z, core),
        "y+": device(x, step(y, 1, 4), z, core),
        "y-": device(x, step(y, -1, 4), z, core),
        "z+": device(x, y, step(z, 1, 8), core),
        "z-": device(x, y, step(z, -1, 8), core),
        "s": device(x, y, z, 1 - core),
    }
    query_group = {
        b: device(x_pair if dx else x, step(y, dy, 4), z, core) for b, (dy, dx) in DELTA.items()
    }
    x_far = step(x, 2, 4)
    four = [device(x_far, y, z, core), device(x, y, z, 1 - core), device(x_far, y, z, 1 - core)]
    column_group = [device(x, y, step(z, d, 8), core) for d in range(1, 8)]

    half_pool = POOL // 2
    pool_copies = [
        pltpu.make_async_copy(
            pool_ref.at[pl.ds(h * half_pool, half_pool)],
            pool.at[pl.ds(h * half_pool, half_pool)],
            local_sem.at[h],
        )
        for h in range(2)
    ]
    own_copy = pltpu.make_async_copy(q_ref, allq.at[pl.ds(0, BLOCK)], local_sem.at[2])
    own_copy.start()
    for c in pool_copies:
        c.start()

    barrier = pltpu.get_barrier_semaphore()
    partners = list(query_group.values()) + four + column_group
    partners += [device(lax.rem(x_pair + 2, 4), y, z, core)]
    for p in partners:
        pl.semaphore_signal(barrier, inc=1, device_id=p, device_id_type=MESH)
    pl.semaphore_wait(barrier, len(partners))

    def pick_col(if_odd, if_even):
        return pl.multiple_of((if_even + odd * (if_odd - if_even)) * TILE, TILE)

    IN = {
        "0": (0, 28, 4), "1": (4, 24, 4), "2": (8, 20, 4), "3": (12, 16, 4), "4": (16, 12, 4),
        "4a": (16, 12, 2), "4b": (18, 14, 2), "01": (0, 24, 8), "23": (8, 16, 8), "012": (0, 20, 12),
        "E": (0, 16, 16), "L": (16, 0, 16),
        "z0": (28, 0, 4), "z1": (24, 4, 4), "z2": (20, 8, 4),
    }

    copies = {}
    made = []

    def send(name, to, src_block, dst_block, cols, rows=(0, 64)):
        if_odd, if_even, tiles = IN[cols]
        width = pl.ds(pick_col(if_odd, if_even), tiles * TILE)
        first = pl.multiple_of(core * 64 + rows[0], 32)
        src = q_ref if src_block == OWN else allq
        n = len(made)
        c = pltpu.make_async_remote_copy(
            src_ref=src.at[pl.ds(pl.multiple_of(src_block * BLOCK + first, 32), rows[1]), width],
            dst_ref=allq.at[pl.ds(pl.multiple_of(dst_block * BLOCK + first, 32), rows[1]), width],
            send_sem=send_sem.at[n],
            recv_sem=recv_sem.at[n],
            device_id=target[to],
            device_id_type=MESH,
        )
        made.append(c)
        copies[name] = c
        c.start()

    def send_small(name, src, dst, to):
        n = len(made)
        c = pltpu.make_async_remote_copy(
            src_ref=src, dst_ref=dst, send_sem=send_sem.at[n], recv_sem=recv_sem.at[n],
            device_id=to, device_id_type=MESH,
        )
        made.append(c)
        copies[name] = c
        c.start()

    def got(*names):
        for name in names:
            copies.pop(name).wait_recv()

    def along_z(block, cols):
        send(f"z+{block}{cols}", "z+", block, block, cols, (0, 32))
        send(f"z-{block}{cols}", "z-", block, block, cols, (32, 32))

    def got_z(block, *cols):
        for c in cols:
            got(f"z+{block}{c}", f"z-{block}{c}")

    def share(block, part):
        send(f"s{block}{part}", "s", block, block, part)

    def got_share(block, part):
        got(f"s{block}{part}")

    def score(pair, part):
        if_odd, if_even, tiles = IN[part]
        width = pl.ds(pick_col(if_odd, if_even), tiles * TILE)
        rows = pl.ds(pair * 2 * BLOCK, 2 * BLOCK)
        s = dot(allq[rows, width], pool[:, width])
        if part == "E":
            scores[rows, :] = s
        else:
            scores[rows, :] = scores[rows, :] + s

    send("YP0", "y-", OWN, YP, "0")
    send("YM0", "y+", OWN, YM, "0")
    send("X01", "x+", OWN, X, "01")
    send("X23", "x-", OWN, X, "23")
    send("YP1", "y-", OWN, YP, "1")
    send("YM1", "y+", OWN, YM, "1")
    send("X4a", "x+", OWN, X, "4a")
    send("X4b", "x-", OWN, X, "4b")
    for k in "234":
        send("YP" + k, "y-", OWN, YP, k)
        send("YM" + k, "y+", OWN, YM, k)

    def onward(k):
        got("YP" + k, "YM" + k)
        send("XP" + k, "x+", YP, XP, k)
        send("XM" + k, "x-", YM, XM, k)

    onward("0")

    for c in pool_copies:
        c.wait()
    pick = pick_ref[0]
    near = pool.reshape(POOL // 16, 16, D)[lax.div(pick, 16)].astype(jnp.float32)
    is_pick = lax.broadcasted_iota(jnp.int32, (16, D), 0) == lax.rem(pick, 16)
    row = jnp.sum(jnp.where(is_pick, near, 0.0), axis=0, keepdims=True)
    for i in range(D // TILE):
        pick_f32[pl.ds(i, 1), :] = row[:, i * TILE : (i + 1) * TILE]
    pick_buf[pl.ds(0, 32), :] = pick_f32[pl.ds(0, 32), :].astype(jnp.bfloat16)
    back = {X: X, YP: YM, YM: YP, XP: XM, XM: XP, Y2: Y2, X2: X2}
    for b, to in query_group.items():
        send_small(f"p{b}", pick_buf.at[pl.ds(0, 32)], pick_buf.at[pl.ds(back[b] * 32, 32)], to)

    got("X01", "X23")
    share(X, "E")
    along_z(X, "01")
    along_z(X, "2")
    onward("1")
    along_z(YP, "01")
    along_z(YM, "01")
    onward("2")
    along_z(YP, "2")
    along_z(YM, "2")

    own_copy.wait()
    got(*[f"p{b}" for b in query_group])
    pick_f32[...] = pick_buf[...].astype(jnp.float32)
    for i in range(D // TILE):
        pick_rows[:, pl.ds(i * TILE, TILE)] = pick_f32[pl.ds(i, 8, stride=32), :]
    eight = pick_rows[...].astype(jnp.bfloat16)
    sims = dot(jnp.concatenate([eight, eight], axis=0), allq[pl.ds(0, BLOCK), :])
    best = jnp.broadcast_to(jnp.max(sims, axis=0, keepdims=True), (8, TILE))
    cover_x[pl.ds(0, 8), :] = best
    for i, to in enumerate(four):
        send_small(f"cx{i}", cover_x.at[pl.ds(0, 8)], cover_x.at[pl.ds(8 + 8 * i, 8)], to)

    got_share(X, "E")
    score(0, "E")

    onward("3")
    send("Y2a", "y-", YP, Y2, "01")
    send("Y2b", "y+", YM, Y2, "23")
    share(YP, "E")
    share(YM, "E")
    onward("4")
    send("Y2c", "y-", YP, Y2, "4a")
    send("Y2d", "y+", YM, Y2, "4b")

    got("cx0", "cx1", "cx2")
    best = jnp.maximum(
        jnp.maximum(cover_x[pl.ds(0, 8), :], cover_x[pl.ds(8, 8), :]),
        jnp.maximum(cover_x[pl.ds(16, 8), :], cover_x[pl.ds(24, 8), :]),
    )
    cover_z[pl.ds(0, 8), :] = best
    for i, to in enumerate(column_group):
        send_small(f"cz{i}", cover_z.at[pl.ds(0, 8)], cover_z.at[pl.ds(8 + 8 * i, 8)], to)

    got("XP0", "XM0", "XP1", "XM1")
    got("X4a", "X4b")
    got_z(X, "01", "2")
    share(X, "L")
    got_share(YP, "E")
    got_share(YM, "E")
    score(1, "E")
    got("XP2", "XM2")
    along_z(XP, "012")
    along_z(XM, "012")
    got("Y2a", "Y2b")
    send("X2a", "x+", Y2, X2, "0")
    send("X2b", "x-", Y2, X2, "2")
    send("X2c", "y-", XP, X2, "1")
    along_z(Y2, "012")
    share(Y2, "E")
    got_z(YP, "01", "2")
    got_z(YM, "01", "2")
    share(YP, "L")
    share(YM, "L")
    got_share(X, "L")
    score(0, "L")
    got("XP3", "XM3")
    send("X2d", "y+", XM, X2, "3")
    share(XP, "E")
    share(XM, "E")

    got(*[f"cz{i}" for i in range(7)])
    best = cover_z[pl.ds(0, 8), :]
    for i in range(7):
        best = jnp.maximum(best, cover_z[pl.ds(8 + 8 * i, 8), :])
    cover_q[pl.ds(0, 8), :] = best
    cover_ref[...] = best
    for b, to in query_group.items():
        send_small(f"cq{b}", cover_q.at[pl.ds(0, 8)], cover_q.at[pl.ds(back[b] * 8, 8)], to)

    got("XP4", "XM4", "Y2c", "Y2d")
    got_share(YP, "L")
    got_share(YM, "L")
    score(1, "L")
    got_z(Y2, "012")
    send("X2e", "x+", Y2, X2, "z0")
    send("X2f", "x-", Y2, X2, "z1")
    share(Y2, "L")
    got_z(XP, "012")
    got_z(XM, "012")
    send("X2g", "y-", XP, X2, "z2")
    send("X2h", "y+", XM, X2, "4")
    share(XP, "L")
    share(XM, "L")
    got_share(XP, "E")
    got_share(XM, "E")
    score(2, "E")
    got("X2a", "X2b", "X2c", "X2d")
    share(X2, "E")
    got_share(XP, "L")
    got_share(XM, "L")
    score(2, "L")
    got("X2e", "X2f", "X2g", "X2h")
    share(X2, "L")
    got_share(Y2, "E")
    got_share(X2, "E")
    score(3, "E")

    got(*[f"cq{b}" for b in query_group])
    rows = jnp.concatenate(
        [cover_q[pl.ds(8 * b, 1), :] for b in range(8)] + [jnp.zeros((TILE - 8, TILE), jnp.float32)], axis=0
    )
    turned = rows.T
    for b in range(8):
        columns[pl.ds(b * BLOCK, BLOCK), :] = jnp.broadcast_to(turned[:, b : b + 1], (BLOCK, TILE))

    def gain(first, groups, carry):
        def body(g, carry):
            summed, highest = carry
            r = pl.ds(pl.multiple_of(first + g * 8, 8), 8)
            s = scores[r, :]
            c = jnp.concatenate([columns[r, :]] * (POOL // TILE), axis=1)
            return summed + jnp.maximum(s - c, 0.0), jnp.maximum(highest, s)

        return lax.fori_loop(0, groups, body, carry)

    start = (jnp.zeros((8, POOL), jnp.float32), jnp.full((8, POOL), -jnp.inf, jnp.float32))
    carry = gain(0, 6 * BLOCK // 8, start)
    part_ref[pl.ds(0, 8), :] = carry[0]
    part_ref[pl.ds(8, 8), :] = carry[1]
    got_share(Y2, "L")
    got_share(X2, "L")
    score(3, "L")
    carry = gain(6 * BLOCK, 2 * BLOCK // 8, (part_ref[pl.ds(0, 8), :], part_ref[pl.ds(8, 8), :]))
    part_ref[pl.ds(0, 8), :] = carry[0]
    part_ref[pl.ds(8, 8), :] = carry[1]
    for c in made:
        c.wait_send()


COPIES = 100


def choose(part_ref, cover_ref, ids_ref, gains_ref, out_cover_ref):
    summed = jnp.sum(part_ref[pl.ds(0, 8), :], axis=0, keepdims=True)
    highest = jnp.max(part_ref[pl.ds(8, 8), :], axis=0, keepdims=True)
    gain = summed * SCALE + 1.0 * (highest * SCALE)
    ids = ids_ref[...]
    lane, group = jnp.bitwise_and(ids, TILE - 1), jnp.right_shift(ids, 7)
    out = jnp.zeros(ids.shape, jnp.float32)
    for k in range(POOL // TILE):
        row = jnp.broadcast_to(gain[:, k * TILE : (k + 1) * TILE], ids.shape)
        out = jnp.where(group == k, jnp.take_along_axis(row, lane, axis=1, mode="promise_in_bounds"), out)
    gains_ref[...] = out
    out_cover_ref[...] = cover_ref[pl.ds(0, 1), :] * SCALE


def on_device(pool, cand_ids, pick_ids, queries):
    f32, bf16 = jnp.float32, jnp.bfloat16
    vmem = pl.BlockSpec(memory_space=pltpu.VMEM)
    part, cover = pl.pallas_call(
        gather_and_score,
        name="gather_and_score",
        out_shape=(jax.ShapeDtypeStruct((16, POOL), f32), jax.ShapeDtypeStruct((8, TILE), f32)),
        in_specs=[
            pl.BlockSpec(memory_space=pltpu.SMEM),
            pl.BlockSpec(memory_space=pl.ANY),
            pl.BlockSpec(memory_space=pl.ANY),
        ],
        out_specs=(vmem, vmem),
        scratch_shapes=[
            pltpu.VMEM((8 * BLOCK, D), bf16),
            pltpu.VMEM((POOL, D), bf16),
            pltpu.VMEM((8 * BLOCK, POOL), f32),
            pltpu.VMEM((256, TILE), f32),
            pltpu.VMEM((256, TILE), bf16),
            pltpu.VMEM((8, D), f32),
            pltpu.VMEM((32, TILE), f32),
            pltpu.VMEM((64, TILE), f32),
            pltpu.VMEM((64, TILE), f32),
            pltpu.VMEM((8 * BLOCK, TILE), f32),
            pltpu.SemaphoreType.DMA((3,)),
            pltpu.SemaphoreType.DMA((COPIES,)),
            pltpu.SemaphoreType.DMA((COPIES,)),
        ],
        compiler_params=pltpu.CompilerParams(
            collective_id=0, has_side_effects=True, vmem_limit_bytes=60 << 20
        ),
        cost_estimate=pl.CostEstimate(
            flops=2 * POOL * 1024 * D, bytes_accessed=POOL * D * 2, transcendentals=0
        ),
    )(pick_ids, pool, queries)
    gains, own_cover = pl.pallas_call(
        choose,
        name="choose",
        out_shape=(jax.ShapeDtypeStruct((8, TILE), f32), jax.ShapeDtypeStruct((1, TILE), f32)),
        in_specs=[vmem, vmem, vmem],
        out_specs=(vmem, vmem),
    )(part, cover, cand_ids.reshape(8, TILE))
    return gains.reshape(-1), own_cover.reshape(-1)


def solution(mesh):
    in_specs = (
        P(("cand", "query"), None),
        P(("cand", "query")),
        P(("cand", "query")),
        P("query", None),
    )
    out_specs = (P(("cand", "query")), P("query"))
    return jax.shard_map(
        on_device, mesh=mesh, in_specs=in_specs, out_specs=out_specs, check_vma=False
    )
```

time: 290 us -> 51.1 us (0.18)
  waiting for transfers between devices: 155 us -> 0 us
  blocking collectives: 77 us -> 0 us
  Pallas kernels: 0 us -> 49.7 us
  local copies, waits for them, and re-layouts: 21 us -> 0 us
  matrix products: 20 us -> 0 us
  between operations: 14.7 us -> 1.28 us
    all_gather x1 -> x0, waiting for transfers between devices: 155 us -> none  [on_device(): lax.all_gather(queries, 'query', axis=0, tiled=True)]
    pmax x1 -> x0, blocking collectives: 77 us -> none  [on_device(): coverage = lax.pmax(best, ('cand', 'query'))]
    pallas_call x0 -> x2, Pallas kernels: none -> 49.7 us  [the longest x1 48.1 us: on_device(): pl.pallas_call(gather_and_score, name='gather_and_score', out_shape=(jax....]
    gather x1 -> x0, local copies, waits for them, and re-layouts: 20.4 us -> none  [on_device(): candidates = jnp.take(pool, cand_ids, axis=0)]
    dot_general x2 -> x0, matrix products: 20 us -> none  [similarity(): lax.dot_general(rows, targets, (((1,), (1,)), ((), ())), preferred_elemen...]
  transfers between devices with their start and end apart: 1 -> 0, of which waited for: 1 -> 0; matrix products, arithmetic and copies ran while one was open for 7% -> 0% of each run, Pallas kernels for 0% -> 0%
where the time goes in v1:
time: 51.1 us; the launch traced here: 50.9 us
  Pallas kernels  49.7 us (97%)
  between operations  1.28 us (3%)
    pallas_call x1, Pallas kernels, on_device(): pl.pallas_call(gather_and_score, name='gather_and_score', out_shape=(jax....  48.1 us
    pallas_call x1, Pallas kernels, on_device(): pl.pallas_call(choose, name='choose', out_shape=(jax.ShapeDtypeStruct((8,...  1.58 us

profile of v1, /device:TPU:1, one launch (start us, length us, event | category | flops | bytes accessed | tf_op | source)
XLA Modules:
  0.0 50.9 jit_solution(13318559891349100623)
XLA Ops:
  1.3 48.1 %gather_and_score.1 = (f32[16,1280]{1,0:T(8,128)}, f32[8,128]{1,0:T(8,128)}) custom-call(s32[1]{0:T(128)S(6)} %copy.6.pick_ref, bf16[1280,4096]{1,0:T(8,128)(2,1)} %pool_ref.1, bf16[128,4096]{1,0:T(8,128)(2,1)} %q_ref.1), custom_call_target="tpu_custom_call" | custom-call | flops 10737418240 | bytes 10485760 | tf_op jit(solution)/shard_map/gather_and_score/pallas_call | solution.py:343
  49.4 1.6 %choose.1 = (f32[8,128]{1,0:T(8,128)}, f32[1,128]{1,0:T(1,128)}) custom-call(f32[16,1280]{1,0:T(8,128)} %get-tuple-element.6.part_ref, f32[8,128]{1,0:T(8,128)} %get-tuple-element.7.cover_ref, s32[8,128]{1,0:T(8,128)} %bitcast.3), custom_call_target="tpu_custom_call" | custom-call | tf_op jit(solution)/shard_map/choose/pallas_call | solution.py:375

commit v2 on v0

v2 whole, which is shorter than its diff:
```python
import jax
import jax.numpy as jnp
from jax import lax
from jax.experimental import pallas as pl
from jax.experimental.pallas import tpu as pltpu
from jax.sharding import PartitionSpec as P

MESH = pl.DeviceIdType.MESH
D = 4096
TILE = 128
BLOCK = 128
POOL = 1280
SCALE = 1.0 / 64.0
SMALL = ["", "p", "cx", "cz", "cq"]
OWN, X, YP, YM, XP, XM, Y2, X2 = range(8)
DELTA = {X: (0, 1), YP: (1, 0), YM: (3, 0), XP: (1, 1), XM: (3, 1), Y2: (2, 0), X2: (2, 1)}


def where_am_i():
    cand, query = lax.axis_index("cand"), lax.axis_index("query")
    core = lax.rem(cand, 2)
    x = lax.rem(lax.div(cand, 2), 2) * 2 + lax.rem(query, 2)
    return x, lax.div(query, 2), lax.div(cand, 4), core


def device(x, y, z, core):
    return ((z * 2 + lax.div(x, 2)) * 2 + core, y * 2 + lax.rem(x, 2))


def dot(a, b):
    return lax.dot_general(a, b, (((1,), (1,)), ((), ())), preferred_element_type=jnp.float32)


def gather_and_score(
    pick_ref, pool_ref, q_ref, part_ref, cover_ref,
    allq, pool, scores, pick_f32, pick_buf, pick_rows, cover_x, cover_z, cover_q, columns,
    local_sem, send_sem, recv_sem,
):
    x, y, z, core = where_am_i()
    odd = lax.rem(z, 2)
    x_pair = x + 1 - 2 * lax.rem(x, 2)

    def step(v, by, size):
        return lax.rem(v + by + size, size)

    target = {
        "x+": device(step(x, 1, 4), y, z, core),
        "x-": device(step(x, -1, 4), y, z, core),
        "y+": device(x, step(y, 1, 4), z, core),
        "y-": device(x, step(y, -1, 4), z, core),
        "z+": device(x, y, step(z, 1, 8), core),
        "z-": device(x, y, step(z, -1, 8), core),
        "s": device(x, y, z, 1 - core),
    }
    query_group = {
        b: device(x_pair if dx else x, step(y, dy, 4), z, core) for b, (dy, dx) in DELTA.items()
    }
    x_far = step(x, 2, 4)
    four = [device(x_far, y, z, core), device(x, y, z, 1 - core), device(x_far, y, z, 1 - core)]
    column_group = [device(x, y, step(z, d, 8), core) for d in range(1, 8)]

    half_pool = POOL // 2
    pool_copies = [
        pltpu.make_async_copy(
            pool_ref.at[pl.ds(h * half_pool, half_pool)],
            pool.at[pl.ds(h * half_pool, half_pool)],
            local_sem.at[h],
        )
        for h in range(2)
    ]
    own_copy = pltpu.make_async_copy(q_ref, allq.at[pl.ds(0, BLOCK)], local_sem.at[2])
    own_copy.start()
    for c in pool_copies:
        c.start()

    barrier = pltpu.get_barrier_semaphore()
    partners = list(query_group.values()) + four + column_group
    partners += [device(lax.rem(x_pair + 2, 4), y, z, core)]
    for p in partners:
        pl.semaphore_signal(barrier, inc=1, device_id=p, device_id_type=MESH)
    pl.semaphore_wait(barrier, len(partners))

    def pick_col(if_odd, if_even):
        return pl.multiple_of((if_even + odd * (if_odd - if_even)) * TILE, TILE)

    COLS = {
        "c0": (0, 24, 8), "c1": (8, 16, 8), "c2": (16, 8, 8), "cz": (24, 0, 8),
        "c2a": (16, 8, 4), "c2b": (20, 12, 4), "cza": (24, 0, 4), "czb": (28, 4, 4), "e": (0, 16, 16), "l": (16, 0, 16), "all": (0, 0, 32),
    }

    groups = {}
    sent = [0]

    def send(group, to, src_block, dst_block, cols, rows=(0, 64)):
        if_odd, if_even, tiles = COLS[cols]
        width = pl.ds(pick_col(if_odd, if_even), tiles * TILE)
        first = pl.multiple_of(core * 64 + rows[0], 32)
        src = q_ref if src_block == OWN else allq
        n = groups.setdefault(group, [len(groups), 0, tiles])
        n[1] += rows[1]
        sent[0] += rows[1] // 32 * tiles
        pltpu.make_async_remote_copy(
            src_ref=src.at[pl.ds(pl.multiple_of(src_block * BLOCK + first, 32), rows[1]), width],
            dst_ref=allq.at[pl.ds(pl.multiple_of(dst_block * BLOCK + first, 32), rows[1]), width],
            send_sem=send_sem.at[0],
            recv_sem=recv_sem.at[n[0]],
            device_id=target[to],
            device_id_type=MESH,
        ).start()

    def send_small(group, src, dst, to):
        n = groups.setdefault(group, [len(groups), 0, 1])
        pltpu.make_async_remote_copy(
            src_ref=src, dst_ref=dst, send_sem=send_sem.at[SMALL.index(group)], recv_sem=recv_sem.at[n[0]],
            device_id=to, device_id_type=MESH,
        ).start()

    def got(*names):
        for group in names:
            n, rows, tiles = groups[group]
            ref = allq.at[pl.ds(0, rows), pl.ds(0, tiles * TILE)]
            pltpu.make_async_copy(ref, ref, recv_sem.at[n]).wait()

    def all_small(group, ref, rows):
        ref = ref.at[pl.ds(0, rows)]
        return pltpu.make_async_copy(ref, ref, recv_sem.at[groups[group][0]])

    def along_z(group, block, cols):
        send(group, "z+", block, block, cols, (0, 32))
        send(group, "z-", block, block, cols, (32, 32))

    def share(group, part, *blocks):
        for block in blocks:
            send(group, "s", block, block, part)

    def score(step):
        rows = pl.ds(pl.multiple_of((2 * lax.div(step, 4) + lax.rem(step, 2)) * 2 * BLOCK, 2 * BLOCK), 2 * BLOCK)
        late = lax.div(lax.rem(step, 4), 2)
        width = pl.ds(pl.multiple_of(lax.rem(late + 1 + odd, 2) * (D // 2), D // 2), D // 2)
        scores[rows, :] = scores[rows, :] + dot(allq[rows, width], pool[:, width])

    def gain(first, groups, carry):
        def body(g, carry):
            summed, highest = carry
            r = pl.ds(pl.multiple_of(first + g * 8, 8), 8)
            s = scores[r, :]
            c = jnp.concatenate([columns[r, :]] * (POOL // TILE), axis=1)
            return summed + jnp.maximum(s - c, 0.0), jnp.maximum(highest, s)

        return lax.fori_loop(0, groups, body, carry)

    send("Y0", "y-", OWN, YP, "c0")
    send("Y0", "y+", OWN, YM, "c0")
    send("X", "x+", OWN, X, "c0")
    send("X", "x-", OWN, X, "c1")

    own_copy.wait()
    for c in pool_copies:
        c.wait()
    pick = pick_ref[0]
    near = pool.reshape(POOL // 16, 16, D)[lax.div(pick, 16)].astype(jnp.float32)
    is_pick = lax.broadcasted_iota(jnp.int32, (16, D), 0) == lax.rem(pick, 16)
    row = jnp.sum(jnp.where(is_pick, near, 0.0), axis=0, keepdims=True)
    for i in range(D // TILE):
        pick_f32[pl.ds(i, 1), :] = row[:, i * TILE : (i + 1) * TILE]
    pick_buf[pl.ds(0, 32), :] = pick_f32[pl.ds(0, 32), :].astype(jnp.bfloat16)
    back = {X: X, YP: YM, YM: YP, XP: XM, XM: XP, Y2: Y2, X2: X2}
    for b, to in query_group.items():
        send_small("p", pick_buf.at[pl.ds(0, 32)], pick_buf.at[pl.ds(back[b] * 32, 32)], to)

    for k in "12":
        send("Y" + k, "y-", OWN, YP, "c" + k)
        send("Y" + k, "y+", OWN, YM, "c" + k)

    def clear(g, _):
        scores[pl.ds(pl.multiple_of(g * 8, 8), 8), :] = jnp.zeros((8, POOL), jnp.float32)
        return 0

    lax.fori_loop(0, 8 * BLOCK // 8, clear, 0)

    def before_0():
        got("Y0")
        send("XP0", "x+", YP, XP, "c0")
        send("XP0", "x-", YM, XM, "c0")
        along_z("zY", YP, "c0")
        along_z("zY", YM, "c0")
        got("X")
        share("sXe", "e", X)
        along_z("zX", X, "e")
        all_small("p", pick_buf, 7 * 32).wait()
        pick_f32[...] = pick_buf[...].astype(jnp.float32)
        for i in range(D // TILE):
            pick_rows[:, pl.ds(i * TILE, TILE)] = pick_f32[pl.ds(i, 8, stride=32), :]
        eight = pick_rows[...].astype(jnp.bfloat16)
        sims = dot(jnp.concatenate([eight, eight], axis=0), allq[pl.ds(0, BLOCK), :])
        cover_x[pl.ds(0, 8), :] = jnp.broadcast_to(jnp.max(sims, axis=0, keepdims=True), (8, TILE))
        for i, to in enumerate(four):
            send_small("cx", cover_x.at[pl.ds(0, 8)], cover_x.at[pl.ds(8 + 8 * i, 8)], to)
        got("Y1")
        send("XP1", "x+", YP, XP, "c1")
        send("XP1", "x-", YM, XM, "c1")
        share("sYe", "e", YP, YM)
        send("Y2e", "y-", YP, Y2, "c0")
        send("Y2e", "y+", YM, Y2, "c1")
        got("sXe")

    def before_1():
        got("zY")
        send("XPz", "x+", YP, XP, "cz")
        send("XPz", "x-", YM, XM, "cz")
        got("Y2")
        send("XP2", "x+", YP, XP, "c2")
        send("XP2", "x-", YM, XM, "c2")
        send("Y2l", "y-", YP, Y2, "cz")
        send("Y2l", "y+", YM, Y2, "c2")
        share("sYl", "l", YP, YM)
        got("zX")
        share("sXl", "l", X)
        got("sYe")

    def before_2():
        got("XP0", "XP1")
        send("X2e", "y-", XP, X2, "c0")
        send("X2e", "y+", XM, X2, "c1")
        share("sXPe", "e", XP, XM)
        got("Y2e")
        share("sY2e", "e", Y2)
        all_small("cx", cover_x, 24).wait()
        best = jnp.maximum(
            jnp.maximum(cover_x[pl.ds(0, 8), :], cover_x[pl.ds(8, 8), :]),
            jnp.maximum(cover_x[pl.ds(16, 8), :], cover_x[pl.ds(24, 8), :]),
        )
        cover_z[pl.ds(0, 8), :] = best
        for i, to in enumerate(column_group):
            send_small("cz", cover_z.at[pl.ds(0, 8)], cover_z.at[pl.ds(8 + 8 * i, 8)], to)
        got("sXl")

    def before_3():
        got("sYl")

    def before_4():
        got("Y2l")
        send("X2l", "x+", Y2, X2, "c2a")
        send("X2l", "x-", Y2, X2, "c2b")
        got("XPz")
        send("X2l", "y-", XP, X2, "cza")
        send("X2l", "y+", XM, X2, "czb")
        share("sY2l", "l", Y2)
        got("sXPe")

    def before_5():
        all_small("cz", cover_z, 56).wait()
        best = cover_z[pl.ds(0, 8), :]
        for i in range(7):
            best = jnp.maximum(best, cover_z[pl.ds(8 + 8 * i, 8), :])
        cover_q[pl.ds(0, 8), :] = best
        cover_ref[...] = best
        for b, to in query_group.items():
            send_small("cq", cover_q.at[pl.ds(0, 8)], cover_q.at[pl.ds(back[b] * 8, 8)], to)
        got("XP2")
        share("sXPl", "l", XP, XM)
        got("X2e")
        share("sX2e", "e", X2)
        got("sY2e", "sX2e")

    def before_6():
        got("X2l")
        share("sX2l", "l", X2)
        got("sXPl")

    def before_7():
        all_small("cq", cover_q, 56).wait()
        rows = jnp.concatenate(
            [cover_q[pl.ds(8 * b, 1), :] for b in range(8)] + [jnp.zeros((TILE - 8, TILE), jnp.float32)], axis=0
        )
        turned = rows.T
        for b in range(8):
            columns[pl.ds(b * BLOCK, BLOCK), :] = jnp.broadcast_to(turned[:, b : b + 1], (BLOCK, TILE))
        start = (jnp.zeros((8, POOL), jnp.float32), jnp.full((8, POOL), -jnp.inf, jnp.float32))
        summed, highest = gain(0, 6 * BLOCK // 8, start)
        part_ref[pl.ds(0, 8), :] = summed
        part_ref[pl.ds(8, 8), :] = highest
        got("sY2l", "sX2l")

    before = [before_0, before_1, before_2, before_3, before_4, before_5, before_6, before_7]

    def one_step(step, _):
        for k, segment in enumerate(before):
            pl.when(step == k)(segment)
        score(step)
        return 0

    lax.fori_loop(0, len(before), one_step, 0)

    summed, highest = gain(6 * BLOCK, 2 * BLOCK // 8, (part_ref[pl.ds(0, 8), :], part_ref[pl.ds(8, 8), :]))
    part_ref[pl.ds(0, 8), :] = summed
    part_ref[pl.ds(8, 8), :] = highest

    wide, rest = divmod(sent[0], 8 * BLOCK // 32)
    for n, tiles in ((8 * BLOCK, wide), (rest * 32, 1)):
        if n and tiles:
            ref = allq.at[pl.ds(0, n), pl.ds(0, tiles * TILE)]
            pltpu.make_async_copy(ref, ref, send_sem.at[0]).wait()
    for group, buffer, rows in (("p", pick_buf, 224), ("cx", cover_x, 24), ("cz", cover_z, 56), ("cq", cover_q, 56)):
        ref = buffer.at[pl.ds(0, rows)]
        pltpu.make_async_copy(ref, ref, send_sem.at[SMALL.index(group)]).wait()


def choose(part_ref, cover_ref, ids_ref, gains_ref, out_cover_ref):
    summed = jnp.sum(part_ref[pl.ds(0, 8), :], axis=0, keepdims=True)
    highest = jnp.max(part_ref[pl.ds(8, 8), :], axis=0, keepdims=True)
    gain = summed * SCALE + 1.0 * (highest * SCALE)
    ids = ids_ref[...]
    lane, group = jnp.bitwise_and(ids, TILE - 1), jnp.right_shift(ids, 7)
    out = jnp.zeros(ids.shape, jnp.float32)
    for k in range(POOL // TILE):
        row = jnp.broadcast_to(gain[:, k * TILE : (k + 1) * TILE], ids.shape)
        out = jnp.where(group == k, jnp.take_along_axis(row, lane, axis=1, mode="promise_in_bounds"), out)
    gains_ref[...] = out
    out_cover_ref[...] = cover_ref[pl.ds(0, 1), :] * SCALE


def on_device(pool, cand_ids, pick_ids, queries):
    f32, bf16 = jnp.float32, jnp.bfloat16
    vmem = pl.BlockSpec(memory_space=pltpu.VMEM)
    part, cover = pl.pallas_call(
        gather_and_score,
        name="gather_and_score",
        out_shape=(jax.ShapeDtypeStruct((16, POOL), f32), jax.ShapeDtypeStruct((8, TILE), f32)),
        in_specs=[
            pl.BlockSpec(memory_space=pltpu.SMEM),
            pl.BlockSpec(memory_space=pl.ANY),
            pl.BlockSpec(memory_space=pl.ANY),
        ],
        out_specs=(vmem, vmem),
        scratch_shapes=[
            pltpu.VMEM((8 * BLOCK, D), bf16),
            pltpu.VMEM((POOL, D), bf16),
            pltpu.VMEM((8 * BLOCK, POOL), f32),
            pltpu.VMEM((256, TILE), f32),
            pltpu.VMEM((256, TILE), bf16),
            pltpu.VMEM((8, D), f32),
            pltpu.VMEM((32, TILE), f32),
            pltpu.VMEM((64, TILE), f32),
            pltpu.VMEM((64, TILE), f32),
            pltpu.VMEM((8 * BLOCK, TILE), f32),
            pltpu.SemaphoreType.DMA((3,)),
            pltpu.SemaphoreType.DMA((len(SMALL),)),
            pltpu.SemaphoreType.DMA((40,)),
        ],
        compiler_params=pltpu.CompilerParams(
            collective_id=0, has_side_effects=True, vmem_limit_bytes=60 << 20
        ),
        cost_estimate=pl.CostEstimate(
            flops=2 * POOL * 1024 * D, bytes_accessed=POOL * D * 2, transcendentals=0
        ),
    )(pick_ids, pool, queries)
    gains, own_cover = pl.pallas_call(
        choose,
        name="choose",
        out_shape=(jax.ShapeDtypeStruct((8, TILE), f32), jax.ShapeDtypeStruct((1, TILE), f32)),
        in_specs=[vmem, vmem, vmem],
        out_specs=(vmem, vmem),
    )(part, cover, cand_ids.reshape(8, TILE))
    return gains.reshape(-1), own_cover.reshape(-1)


def solution(mesh):
    in_specs = (
        P(("cand", "query"), None),
        P(("cand", "query")),
        P(("cand", "query")),
        P("query", None),
    )
    out_specs = (P(("cand", "query")), P("query"))
    return jax.shard_map(
        on_device, mesh=mesh, in_specs=in_specs, out_specs=out_specs, check_vma=False
    )
```

time: 290 us -> 44.8 us (0.15)
  waiting for transfers between devices: 155 us -> 0 us
  blocking collectives: 77 us -> 0 us
  Pallas kernels: 0 us -> 43.4 us
  local copies, waits for them, and re-layouts: 21 us -> 0 us
  matrix products: 20 us -> 0 us
  between operations: 14.7 us -> 1.28 us
    all_gather x1 -> x0, waiting for transfers between devices: 155 us -> none  [on_device(): lax.all_gather(queries, 'query', axis=0, tiled=True)]
    pmax x1 -> x0, blocking collectives: 77 us -> none  [on_device(): coverage = lax.pmax(best, ('cand', 'query'))]
    pallas_call x0 -> x2, Pallas kernels: none -> 43.4 us  [the longest x1 41.8 us: on_device(): pl.pallas_call(gather_and_score, name='gather_and_score', out_shape=(jax....]
    gather x1 -> x0, local copies, waits for them, and re-layouts: 20.4 us -> none  [on_device(): candidates = jnp.take(pool, cand_ids, axis=0)]
    dot_general x2 -> x0, matrix products: 20 us -> none  [similarity(): lax.dot_general(rows, targets, (((1,), (1,)), ((), ())), preferred_elemen...]
  transfers between devices with their start and end apart: 1 -> 0, of which waited for: 1 -> 0; matrix products, arithmetic and copies ran while one was open for 7% -> 0% of each run, Pallas kernels for 0% -> 0%
where the time goes in v2:
time: 44.8 us; the launch traced here: 44.7 us
  Pallas kernels  43.4 us (97%)
  between operations  1.28 us (3%)
    pallas_call x1, Pallas kernels, on_device(): pl.pallas_call(gather_and_score, name='gather_and_score', out_shape=(jax....  41.8 us
    pallas_call x1, Pallas kernels, on_device(): pl.pallas_call(choose, name='choose', out_shape=(jax.ShapeDtypeStruct((8,...  1.58 us

profile of v2, /device:TPU:1, one launch (start us, length us, event | category | flops | bytes accessed | tf_op | source)
XLA Modules:
  0.0 44.7 jit_solution(8654861421650674854)
XLA Ops:
  1.3 41.8 %gather_and_score.1 = (f32[16,1280]{1,0:T(8,128)}, f32[8,128]{1,0:T(8,128)}) custom-call(s32[1]{0:T(128)S(6)} %copy.6.pick_ref, bf16[1280,4096]{1,0:T(8,128)(2,1)} %pool_ref.1, bf16[128,4096]{1,0:T(8,128)(2,1)} %q_ref.1), custom_call_target="tpu_custom_call" | custom-call | flops 10737418240 | bytes 10485760 | tf_op jit(solution)/shard_map/gather_and_score/pallas_call | solution.py:326
  43.1 1.6 %choose.1 = (f32[8,128]{1,0:T(8,128)}, f32[1,128]{1,0:T(1,128)}) custom-call(f32[16,1280]{1,0:T(8,128)} %get-tuple-element.6.part_ref, f32[8,128]{1,0:T(8,128)} %get-tuple-element.7.cover_ref, s32[8,128]{1,0:T(8,128)} %bitcast.3), custom_call_target="tpu_custom_call" | custom-call | tf_op jit(solution)/shard_map/choose/pallas_call | solution.py:358

commit v3 on v2

--- a/solution.py
+++ b/solution.py
@@ -85,7 +85,7 @@
 
     COLS = {
         "c0": (0, 24, 8), "c1": (8, 16, 8), "c2": (16, 8, 8), "cz": (24, 0, 8),
-        "c2a": (16, 8, 4), "c2b": (20, 12, 4), "cza": (24, 0, 4), "czb": (28, 4, 4), "e": (0, 16, 16), "l": (16, 0, 16), "all": (0, 0, 32),
+        "c0a": (0, 24, 4), "c0b": (4, 28, 4), "c2a": (16, 8, 4), "c2b": (20, 12, 4), "cza": (24, 0, 4), "czb": (28, 4, 4), "e": (0, 16, 16), "l": (16, 0, 16), "all": (0, 0, 32),
     }
 
     groups = {}
@@ -134,7 +134,9 @@
             send(group, "s", block, block, part)
 
     def score(step):
-        rows = pl.ds(pl.multiple_of((2 * lax.div(step, 4) + lax.rem(step, 2)) * 2 * BLOCK, 2 * BLOCK), 2 * BLOCK)
+        in_pair = lax.rem(step + lax.div(step, 2) * (1 - lax.div(step, 4)), 2)
+        pair = 2 * lax.div(step, 4) + in_pair
+        rows = pl.ds(pl.multiple_of(pair * 2 * BLOCK, 2 * BLOCK), 2 * BLOCK)
         late = lax.div(lax.rem(step, 4), 2)
         width = pl.ds(pl.multiple_of(lax.rem(late + 1 + odd, 2) * (D // 2), D // 2), D // 2)
         scores[rows, :] = scores[rows, :] + dot(allq[rows, width], pool[:, width])
@@ -149,8 +151,9 @@
 
         return lax.fori_loop(0, groups, body, carry)
 
-    send("Y0", "y-", OWN, YP, "c0")
-    send("Y0", "y+", OWN, YM, "c0")
+    for k in "ab":
+        send("Y0" + k, "y-", OWN, YP, "c0" + k)
+        send("Y0" + k, "y+", OWN, YM, "c0" + k)
     send("X", "x+", OWN, X, "c0")
     send("X", "x-", OWN, X, "c1")
 
@@ -179,9 +182,10 @@
     lax.fori_loop(0, 8 * BLOCK // 8, clear, 0)
 
     def before_0():
-        got("Y0")
-        send("XP0", "x+", YP, XP, "c0")
-        send("XP0", "x-", YM, XM, "c0")
+        for k in "ab":
+            got("Y0" + k)
+            send("XP0" + k, "x+", YP, XP, "c0" + k)
+            send("XP0" + k, "x-", YM, XM, "c0" + k)
         along_z("zY", YP, "c0")
         along_z("zY", YM, "c0")
         got("X")
@@ -214,15 +218,15 @@
         send("Y2l", "y-", YP, Y2, "cz")
         send("Y2l", "y+", YM, Y2, "c2")
         share("sYl", "l", YP, YM)
-        got("zX")
-        share("sXl", "l", X)
         got("sYe")
 
     def before_2():
-        got("XP0", "XP1")
+        got("XP0a", "XP0b", "XP1")
         send("X2e", "y-", XP, X2, "c0")
         send("X2e", "y+", XM, X2, "c1")
         share("sXPe", "e", XP, XM)
+        got("zX")
+        share("sXl", "l", X)
         got("Y2e")
         share("sY2e", "e", Y2)
         all_small("cx", cover_x, 24).wait()
@@ -233,10 +237,10 @@
         cover_z[pl.ds(0, 8), :] = best
         for i, to in enumerate(column_group):
             send_small("cz", cover_z.at[pl.ds(0, 8)], cover_z.at[pl.ds(8 + 8 * i, 8)], to)
+        got("sYl")
+
+    def before_3():
         got("sXl")
-
-    def before_3():
-        got("sYl")
 
     def before_4():
         got("Y2l")

time: 44.8 us -> 44.7 us (level)
  no operation moved by 1% of the time
where the time goes in v3:
time: 44.7 us; the launch traced here: 44.6 us
  Pallas kernels  43.3 us (97%)
  between operations  1.28 us (3%)
    pallas_call x1, Pallas kernels, on_device(): pl.pallas_call(gather_and_score, name='gather_and_score', out_shape=(jax....  41.7 us
    pallas_call x1, Pallas kernels, on_device(): pl.pallas_call(choose, name='choose', out_shape=(jax.ShapeDtypeStruct((8,...  1.58 us

profile of v3, /device:TPU:1, one launch (start us, length us, event | category | flops | bytes accessed | tf_op | source)
XLA Modules:
  0.0 44.6 jit_solution(13473114048761532987)
XLA Ops:
  1.3 41.7 %gather_and_score.1 = (f32[16,1280]{1,0:T(8,128)}, f32[8,128]{1,0:T(8,128)}) custom-call(s32[1]{0:T(128)S(6)} %copy.6.pick_ref, bf16[1280,4096]{1,0:T(8,128)(2,1)} %pool_ref.1, bf16[128,4096]{1,0:T(8,128)(2,1)} %q_ref.1), custom_call_target="tpu_custom_call" | custom-call | flops 10737418240 | bytes 10485760 | tf_op jit(solution)/shard_map/gather_and_score/pallas_call | solution.py:330
  43.0 1.6 %choose.1 = (f32[8,128]{1,0:T(8,128)}, f32[1,128]{1,0:T(1,128)}) custom-call(f32[16,1280]{1,0:T(8,128)} %get-tuple-element.6.part_ref, f32[8,128]{1,0:T(8,128)} %get-tuple-element.7.cover_ref, s32[8,128]{1,0:T(8,128)} %bitcast.3), custom_call_target="tpu_custom_call" | custom-call | tf_op jit(solution)/shard_map/choose/pallas_call | solution.py:362
